TPU v7x, 32 devices: a whole 2x2x4 slice. The times are simulated.
32 devices in a mesh: groups: 2 (over y), blk: 4 (over z), chan: 4 (over x, core).
Axes of the slice: x: 2, y: 2, z: 4, core: 2. Of those that a mesh axis runs over, the one named last changes fastest.
Arguments:
- fmap1: bfloat16 [128, 256, 128], P(('groups', 'blk'), 'chan'), parts along dimension 0, may hold values from -6 to 6
- fmap2: bfloat16 [128, 256, 128], P(('groups', 'blk'), 'chan'), parts along dimension 0, may hold values from -6 to 6
- windows: int32 [128, 20], P(('groups', 'blk')), parts along dimension 0, may hold values from 0 to 63, as said below
- live: int32 [128], P(('groups', 'blk')), parts along dimension 0, may hold values from 1 to 20, as said below
- cotangent: bfloat16 [128, 20, 128, 128], P(('groups', 'blk')), parts along dimension 0, may hold values from -6 to 6
Outputs:
- grad_one: float32 [128, 256, 128], P(('groups', 'blk'), 'chan'), parts along dimension 0
- grad_two: float32 [128, 256, 128], P(('groups', 'blk'), 'chan'), parts along dimension 0
There are 2 independent parts, one for each index of `groups`. A program takes and returns all parts, laid end to end along the dimension named above; each array names one. Nothing has to cross between parts.
Inputs may be any that keep to these rules, and one draw needn't show every extreme that they name: `windows`: the ids in one row are distinct; they may name blocks anywhere in the frame. Entries at slots live[b] and beyond are padding and carry no weight. `live`: some block uses all 20 slots.
All inputs are finite; a program needn't handle non-finite values.
Results may differ from a plain program's by a relative error of at most 0.0003.
Values may be sent and summed in bfloat16 or wider, within the bound.
A program may use at most 64 MiB of HBM per device.

v0:
```python
import math
import jax
import jax.numpy as jnp
from jax import lax
from jax.sharding import PartitionSpec as P

C = 256


def body(fmap1, fmap2, windows, live, cotangent):
    blocks, channels, site_count = fmap1.shape
    slot_count = windows.shape[1]
    inv_root = 1.0 / math.sqrt(C)
    slot_mask = (jnp.arange(slot_count, dtype=jnp.int32)[None, :] < live[:, None]).astype(
        jnp.float32
    )
    terms = jnp.einsum("bwij,bci->bwcj", cotangent, fmap1, preferred_element_type=jnp.float32)
    terms = terms * (inv_root * slot_mask)[:, :, None, None]
    flat_terms = terms.reshape(blocks * slot_count, channels * site_count)
    flat_ids = windows.reshape(-1)
    piece = lax.all_gather(fmap2, "blk", axis=0, tiled=True)
    piece_rows = piece.shape[0]
    row_ids = jnp.arange(piece_rows, dtype=jnp.int32)
    picker = (flat_ids[:, None] == row_ids[None, :]).astype(jnp.bfloat16)
    fetched = jnp.dot(
        picker, piece.reshape(piece_rows, channels * site_count), preferred_element_type=jnp.float32
    )
    fetched = fetched.astype(jnp.bfloat16).reshape(blocks, slot_count, channels, site_count)
    row_count = blocks * lax.axis_size("blk")
    row_ids = jnp.arange(row_count, dtype=jnp.int32)
    owner_hot = (row_ids[:, None] == flat_ids[None, :]).astype(jnp.float32)
    summed = jnp.dot(
        owner_hot, flat_terms, preferred_element_type=jnp.float32, precision=lax.Precision.HIGHEST
    )
    grad_two = lax.psum_scatter(
        summed.reshape(row_count, channels, site_count), "blk", scatter_dimension=0, tiled=True
    )
    selected = fetched * slot_mask.astype(jnp.bfloat16)[:, :, None, None]
    grad_one = (
        jnp.einsum("bwij,bwcj->bci", cotangent, selected, preferred_element_type=jnp.float32)
        * inv_root
    )
    return (grad_one, grad_two)


def solution(mesh):
    placed = (
        P(("groups", "blk"), "chan", None),
        P(("groups", "blk"), "chan", None),
        P(("groups", "blk"), None),
        P(("groups", "blk")),
        P(("groups", "blk"), None, None, None),
    )
    return jax.shard_map(
        body,
        mesh=mesh,
        in_specs=placed,
        out_specs=(P(("groups", "blk"), "chan", None), P(("groups", "blk"), "chan", None)),
        check_vma=False,
    )
```

profile of v0, /device:TPU:0, one launch (start us, length us, event | category | flops | bytes accessed | tf_op | source)
XLA Modules:
  0.0 94.8 jit_solution(12129404039623603795)
XLA Ops:
  7.2 0.0 copy-start
  7.2 0.0 all-gather.2.cloned.1.call-start
  7.2 0.7 all-gather.2.cloned.1.call-update
  7.9 0.0 reduce-scatter.2.cloned.1.call-start
  8.0 0.8 eq.28
  8.7 0.7 fusion.20
  9.5 0.0 copy-done
  9.5 4.9 %broadcast_multiply_fusion = f32[16,64,20,128]{3,1,2,0:T(8,128)S(1)} fusion(f32[16,20]{1,0:T(8,128)S(1)} %fusion.20, bf16[16,20,128,128]{3,2,1,0:T(8,128)(2,1)} %param.9, bf16[16,64,128]{2,1,0:T(8,128)(2,1)S(1)} %copy-done), kind=kOutput, calls=%fused_computation.5 | convolution fusion | flops 673710080 | bytes 21234944 | tf_op jit(solution)/shard_map/bwij,bci->bwcj/dot_general | solution.py:17
  14.4 0.0 copy-start.1
  14.4 11.9 %fusion = f32[64,64,128]{2,0,1:T(8,128)} fusion(s32[320]{0:T(512)S(1)} %eq.28, f32[40,8,64,128]{3,2,1,0:T(8,128)S(1)} %bitcast.38), kind=kOutput, calls=%fused_computation.2 | convolution fusion | flops 2013286400 | bytes 12584192 | tf_op jit(solution)/shard_map/dot_general | solution.py:32
  26.3 0.0 reduce-scatter.2.cloned.1.call-update
  26.3 0.0 copy-done.1
  26.3 0.1 convert_convert_fusion
  26.4 13.9 %all-gather.2.cloned.1.call-done = bf16[64,64,128]{2,1,0:T(8,128)(2,1)} async-done(((bf16[16,64,128]{2,1,0:T(8,128)(2,1)}), bf16[64,64,128]{2,1,0:T(8,128)(2,1)}) %all-gather.2.cloned.1.call-update) | async-done | bytes 1048592 | tf_op jit(solution)/shard_map/all_gather | solution.py:21
  40.2 2.8 %fusion.6 = bf16[40,8,64,128]{3,1,2,0:T(8,128)(2,1)S(1)} fusion(bf16[8,8,64,128]{3,2,1,0:T(8,128)(2,1)} %bitcast.40, s32[320]{0:T(512)S(1)} %eq.28), kind=kOutput, calls=%fused_computation.9 | convolution fusion | flops 338186240 | bytes 6292736 | tf_op jit(solution)/shard_map/dot_general | solution.py:25
  43.0 1.7 %copy.16 = bf16[40,8,64,128]{3,2,1,0:T(8,128)(2,1)S(1)} copy(bf16[40,8,64,128]{3,1,2,0:T(8,128)(2,1)S(1)} %fusion.6) | data formatting | bytes 10485760
  44.7 8.9 %fusion.10 = f32[16,64,128]{2,1,0:T(8,128)} fusion(bf16[16,20,128,128]{3,2,1,0:T(8,128)(2,1)} %param.9, bf16[16,20,64,128]{3,2,1,0:T(8,128)(2,1)S(1)} %bitcast.39, bf16[16,20]{1,0:T(8,128)(2,1)S(1)} %convert_convert_fusion), kind=kOutput, calls=%fused_computation.11 | convolution fusion | flops 673841152 | bytes 16253568 | tf_op jit(solution)/shard_map/bwij,bwcj->bci/dot_general | solution.py:40
  53.6 32.3 %reduce-scatter.2.cloned.1.call-done = f32[16,64,128]{2,0,1:T(8,128)} async-done(((f32[64,64,128]{2,0,1:T(8,128)}), f32[16,64,128]{2,0,1:T(8,128)}) %reduce-scatter.2.cloned.1.call-update) | async-done | bytes 524304 | tf_op jit(solution)/shard_map/reduce_scatter | solution.py:35
  85.9 2.0 %copy.11 = f32[16,64,128]{2,1,0:T(8,128)} copy(f32[16,64,128]{2,0,1:T(8,128)} %reduce-scatter.2.cloned.1.call-done) | data formatting | bytes 1048576
Async XLA Ops:
  7.2 2.3 %copy-start = (bf16[16,64,128]{2,1,0:T(8,128)(2,1)S(1)}, bf16[16,64,128]{2,1,0:T(8,128)(2,1)}, u32[]{:S(2)}) copy-start(bf16[16,64,128]{2,1,0:T(8,128)(2,1)} %param.5) | copy-start | bytes 786436
  7.2 33.1 %all-gather.2.cloned.1.call-start = ((), (), s32[]{:S(2)}) async-start(), calls=%async_computation.1 | async-start | bytes 1310720 | tf_op jit(solution)/shard_map/all_gather | solution.py:21
  7.9 78.0 %reduce-scatter.2.cloned.1.call-start = ((), (), s32[]{:S(2)}) async-start(), calls=%async_computation.2 | async-start | bytes 2621440 | tf_op jit(solution)/shard_map/reduce_scatter | solution.py:35
  14.4 11.9 %copy-start.1 = (s32[16]{0:T(128)S(1)}, s32[16]{0:T(128)}, u32[]{:S(2)}) copy-start(s32[16]{0:T(128)} %param.8) | copy-start | bytes 196
Sparse Core Ops, SparseCore 0:
  9.6 30.6 all-gather.1
  42.5 43.3 reduce-scatter.1
where the time goes:
time: 95 us; the launch traced here: 94.8 us
  waiting for transfers between devices  46.9 us (49%)
  matrix products  28.5 us (30%)
  between operations  14.1 us (15%)
  local copies, waits for them, and re-layouts  4.45 us (5%)
    reduce_scatter x1, waiting for transfers between devices, body(): lax.psum_scatter(summed.reshape(row_count, channels, site_count), 'blk',...  32.3 us
    all_gather x1, waiting for transfers between devices, body(): piece = lax.all_gather(fmap2, 'blk', axis=0, tiled=True)  13.9 us
    dot_general x1, matrix products, body(): jnp.dot(owner_hot, flat_terms, preferred_element_type=jnp.float32, precis...  11.9 us
    dot_general x1, matrix products, body(): jnp.einsum('bwij,bwcj->bci', cotangent, selected, preferred_element_type=...  8.92 us
    dot_general x1, matrix products, body(): jnp.einsum('bwij,bci->bwcj', cotangent, fmap1, preferred_element_type=jnp...  4.93 us
    unnamed x6, local copies, waits for them, and re-layouts  3.67 us
    dot_general x1, matrix products, body(): jnp.dot(picker, piece.reshape(piece_rows, channels * site_count), preferr...  2.79 us
  transfers between devices with their start and end apart: 2, of which 2 were waited for; matrix products, arithmetic and copies ran while one was open for 33% of the time, Pallas kernels for 0%

commit v1 on v0

--- a/solution.py
+++ b/solution.py
@@ -18,7 +18,12 @@
     terms = terms * (inv_root * slot_mask)[:, :, None, None]
     flat_terms = terms.reshape(blocks * slot_count, channels * site_count)
     flat_ids = windows.reshape(-1)
-    piece = lax.all_gather(fmap2, "blk", axis=0, tiled=True)
+    ring = [fmap2]
+    for hop in range(3):
+        ring.append(lax.ppermute(ring[-1], "blk", [(dev, (dev + 1) % 4) for dev in range(4)]))
+    piece = jnp.roll(
+        jnp.concatenate(ring[::-1], axis=0), (lax.axis_index("blk") + 1) * ring[0].shape[0], axis=0
+    )
     piece_rows = piece.shape[0]
     row_ids = jnp.arange(piece_rows, dtype=jnp.int32)
     picker = (flat_ids[:, None] == row_ids[None, :]).astype(jnp.bfloat16)

time: 95 us -> 95.6 us (level)
  the two profiles are of different devices: /device:TPU:0 before, /device:TPU:18 now
where the time goes in v1:
time: 95.6 us; the launch traced here: 95.4 us
  waiting for transfers between devices  44 us (46%)
  matrix products  27 us (28%)
  between operations  14.2 us (15%)
  starting transfers between devices  4.75 us (5%)
  local copies, waits for them, and re-layouts  4.68 us (5%)
    ppermute x3, waiting for transfers between devices, body(): lax.ppermute(ring[-1], 'blk', [(dev, (dev + 1) % 4) for dev in range(4)])  44 us
    dot_general x1, matrix products, body(): jnp.dot(owner_hot, flat_terms, preferred_element_type=jnp.float32, precis...  11.9 us
    dot_general x1, matrix products, body(): jnp.einsum('bwij,bwcj->bci', cotangent, selected, preferred_element_type=...  8.64 us
    dot_general x1, matrix products, body(): jnp.einsum('bwij,bci->bwcj', cotangent, fmap1, preferred_element_type=jnp...  4.93 us
    ppermute x3, starting transfers between devices, body(): lax.ppermute(ring[-1], 'blk', [(dev, (dev + 1) % 4) for dev in range(4)])  4.72 us
    unnamed x15, local copies, waits for them, and re-layouts  3.75 us
  transfers between devices with their start and end apart: 4, of which 3 were waited for; matrix products, arithmetic and copies ran while one was open for 13% of the time, Pallas kernels for 0%

profile of v1, /device:TPU:18, one launch (start us, length us, event | category | flops | bytes accessed | tf_op | source)
XLA Modules:
  0.0 95.4 jit_solution(943785006551822791)
XLA Ops:
  7.2 0.0 copy-start
  7.2 0.0 reduce-scatter.2.cloned.1.call-start
  7.2 0.8 eq.31
  8.0 0.7 fusion.20
  8.8 0.0 copy-done
  8.8 4.9 %broadcast_multiply_fusion = f32[16,64,20,128]{3,1,2,0:T(8,128)S(1)} fusion(f32[16,20]{1,0:T(8,128)S(1)} %fusion.20, bf16[16,20,128,128]{3,2,1,0:T(8,128)(2,1)} %param.9, bf16[16,64,128]{2,1,0:T(8,128)(2,1)S(1)} %copy-done), kind=kOutput, calls=%fused_computation.5 | convolution fusion | flops 673710080 | bytes 21234944 | tf_op jit(solution)/shard_map/bwij,bci->bwcj/dot_general | solution.py:17
  13.7 0.0 copy-start.1
  13.7 0.0 copy-start.2
  13.7 11.9 %fusion = f32[64,64,128]{2,0,1:T(8,128)} fusion(s32[320]{0:T(512)S(1)} %eq.31, f32[40,8,64,128]{3,2,1,0:T(8,128)S(1)} %bitcast.38), kind=kOutput, calls=%fused_computation.2 | convolution fusion | flops 2013286400 | bytes 12584192 | tf_op jit(solution)/shard_map/dot_general | solution.py:37
  25.6 0.0 reduce-scatter.2.cloned.1.call-update
  25.6 0.0 copy-done.1
  25.6 1.6 %collective-permute-start = (bf16[16,64,128]{2,1,0:T(8,128)(2,1)S(1)}, bf16[16,64,128]{2,1,0:T(8,128)(2,1)S(1)}, u32[]{:S(2)}, u32[]{:S(2)}) collective-permute-start(bf16[16,64,128]{2,1,0:T(8,128)(2,1)S(1)} %copy-done.1), channel_id=1, source_target_pairs={{0,4},{4,8},{8,12},{12,0},{1,5},{5,9},{9,13},{13,1},{2,6},{6,10},{... | collective-permute-start | bytes 786440 | tf_op jit(solution)/shard_map/ppermute | solution.py:23
  27.2 6.5 %collective-permute-done = bf16[16,64,128]{2,1,0:T(8,128)(2,1)S(1)} collective-permute-done((bf16[16,64,128]{2,1,0:T(8,128)(2,1)S(1)}, bf16[16,64,128]{2,1,0:T(8,128)(2,1)S(1)}, u32[]{:S(2)}, u32[]{:S(2)}) %collective-permute-start) | collective-permute-done | bytes 262176 | tf_op jit(solution)/shard_map/ppermute | solution.py:23
  33.7 1.6 %collective-permute-start.1 = (bf16[16,64,128]{2,1,0:T(8,128)(2,1)S(1)}, bf16[16,64,128]{2,1,0:T(8,128)(2,1)S(1)}, u32[]{:S(2)}, u32[]{:S(2)}) collective-permute-start(bf16[16,64,128]{2,1,0:T(8,128)(2,1)S(1)} %collective-permute-done), channel_id=1, source_target_pairs={{0,4},{4,8},{8,12},{12,0},{1,5},{5,9},{9,13},{13,1},{2,6},{6,10},{... | collective-permute-start | bytes 786440 | tf_op jit(solution)/shard_map/ppermute | solution.py:23
  35.3 18.3 %collective-permute-done.1 = bf16[16,64,128]{2,1,0:T(8,128)(2,1)S(1)} collective-permute-done((bf16[16,64,128]{2,1,0:T(8,128)(2,1)S(1)}, bf16[16,64,128]{2,1,0:T(8,128)(2,1)S(1)}, u32[]{:S(2)}, u32[]{:S(2)}) %collective-permute-start.1) | collective-permute-done | bytes 262176 | tf_op jit(solution)/shard_map/ppermute | solution.py:23
  53.6 1.6 %collective-permute-start.2 = (bf16[16,64,128]{2,1,0:T(8,128)(2,1)S(1)}, bf16[16,64,128]{2,1,0:T(8,128)(2,1)S(1)}, u32[]{:S(2)}, u32[]{:S(2)}) collective-permute-start(bf16[16,64,128]{2,1,0:T(8,128)(2,1)S(1)} %collective-permute-done.1), channel_id=1, source_target_pairs={{0,4},{4,8},{8,12},{12,0},{1,5},{5,9},{9,13},{13,1},{2,6},{6,10},{... | collective-permute-start | bytes 786440 | tf_op jit(solution)/shard_map/ppermute | solution.py:23
  55.2 0.0 copy-done.2
  55.2 0.1 convert_convert_fusion
  55.3 19.2 %collective-permute-done.2 = bf16[16,64,128]{2,1,0:T(8,128)(2,1)S(1)} collective-permute-done((bf16[16,64,128]{2,1,0:T(8,128)(2,1)S(1)}, bf16[16,64,128]{2,1,0:T(8,128)(2,1)S(1)}, u32[]{:S(2)}, u32[]{:S(2)}) %collective-permute-start.2) | collective-permute-done | bytes 262176 | tf_op jit(solution)/shard_map/ppermute | solution.py:23
  74.8 0.1 constant_dynamic-slice_fusion
  74.8 1.6 %fusion.6 = bf16[40,8,64,128]{3,1,2,0:T(8,128)(2,1)S(1)} fusion(bf16[8,8,64,128]{3,2,1,0:T(8,128)(2,1)S(1)} %bitcast.40, s32[320]{0:T(512)S(1)} %eq.31), kind=kOutput, calls=%fused_computation.9 | convolution fusion | flops 338186240 | bytes 6292736 | tf_op jit(solution)/shard_map/dot_general | solution.py:30
  76.4 1.5 %copy.14 = bf16[40,8,64,128]{3,2,1,0:T(8,128)(2,1)S(1)} copy(bf16[40,8,64,128]{3,1,2,0:T(8,128)(2,1)S(1)} %fusion.6) | data formatting | bytes 10485760
  77.9 8.6 %fusion.10 = f32[16,64,128]{2,1,0:T(8,128)} fusion(bf16[16,20,128,128]{3,2,1,0:T(8,128)(2,1)} %param.9, bf16[16,20,64,128]{3,2,1,0:T(8,128)(2,1)S(1)} %bitcast.39, bf16[16,20]{1,0:T(8,128)(2,1)S(1)} %convert_convert_fusion), kind=kOutput, calls=%fused_computation.11 | convolution fusion | flops 673841152 | bytes 16253568 | tf_op jit(solution)/shard_map/bwij,bwcj->bci/dot_general | solution.py:45
  86.6 0.0 reduce-scatter.2.cloned.1.call-done
  86.6 2.0 %copy.9 = f32[16,64,128]{2,1,0:T(8,128)} copy(f32[16,64,128]{2,0,1:T(8,128)} %reduce-scatter.2.cloned.1.call-done) | data formatting | bytes 1048576
  (8 shorter events, 0.3 us)
Async XLA Ops:
  7.2 1.6 %copy-start = (bf16[16,64,128]{2,1,0:T(8,128)(2,1)S(1)}, bf16[16,64,128]{2,1,0:T(8,128)(2,1)}, u32[]{:S(2)}) copy-start(bf16[16,64,128]{2,1,0:T(8,128)(2,1)} %param.5) | copy-start | bytes 786436
  7.2 79.4 %reduce-scatter.2.cloned.1.call-start = ((), (), s32[]{:S(2)}) async-start(), calls=%async_computation.1 | async-start | bytes 2621440 | tf_op jit(solution)/shard_map/reduce_scatter | solution.py:40
  13.7 11.9 %copy-start.1 = (bf16[16,64,128]{2,1,0:T(8,128)(2,1)S(1)}, bf16[16,64,128]{2,1,0:T(8,128)(2,1)}, u32[]{:S(2)}) copy-start(bf16[16,64,128]{2,1,0:T(8,128)(2,1)} %param.6) | copy-start | bytes 786436
  13.7 41.5 %copy-start.2 = (s32[16]{0:T(128)S(1)}, s32[16]{0:T(128)}, u32[]{:S(2)}) copy-start(s32[16]{0:T(128)} %param.8) | copy-start | bytes 196
  25.6 8.1 %collective-permute-start = (bf16[16,64,128]{2,1,0:T(8,128)(2,1)S(1)}, bf16[16,64,128]{2,1,0:T(8,128)(2,1)S(1)}, u32[]{:S(2)}, u32[]{:S(2)}) collective-permute-start(bf16[16,64,128]{2,1,0:T(8,128)(2,1)S(1)} %copy-done.1), channel_id=1, source_target_pairs={{0,4},{4,8},{8,12},{12,0},{1,5},{5,9},{9,13},{13,1},{2,6},{6,10},{... | collective-permute-start | bytes 786440 | tf_op jit(solution)/shard_map/ppermute | solution.py:23
  33.7 19.9 %collective-permute-start.1 = (bf16[16,64,128]{2,1,0:T(8,128)(2,1)S(1)}, bf16[16,64,128]{2,1,0:T(8,128)(2,1)S(1)}, u32[]{:S(2)}, u32[]{:S(2)}) collective-permute-start(bf16[16,64,128]{2,1,0:T(8,128)(2,1)S(1)} %collective-permute-done), channel_id=1, source_target_pairs={{0,4},{4,8},{8,12},{12,0},{1,5},{5,9},{9,13},{13,1},{2,6},{6,10},{... | collective-permute-start | bytes 786440 | tf_op jit(solution)/shard_map/ppermute | solution.py:23
  53.6 20.8 %collective-permute-start.2 = (bf16[16,64,128]{2,1,0:T(8,128)(2,1)S(1)}, bf16[16,64,128]{2,1,0:T(8,128)(2,1)S(1)}, u32[]{:S(2)}, u32[]{:S(2)}) collective-permute-start(bf16[16,64,128]{2,1,0:T(8,128)(2,1)S(1)} %collective-permute-done.1), channel_id=1, source_target_pairs={{0,4},{4,8},{8,12},{12,0},{1,5},{5,9},{9,13},{13,1},{2,6},{6,10},{... | collective-permute-start | bytes 786440 | tf_op jit(solution)/shard_map/ppermute | solution.py:23
Sparse Core Ops, SparseCore 0:
  25.7 55.2 reduce-scatter.1
